TPU v7x, 512 devices: a whole 4x8x8 slice. The times are simulated.
512 devices in a mesh: ctx: 64 (over y_lo, z, x), tp: 8 (over y_hi, core).
Axes of the slice: x: 4, y: 8 (y_hi: 4, y_lo: 2; y = y_hi * 2 + y_lo), z: 8, core: 2. Of those that a mesh axis runs over, the one named last changes fastest.
Arguments:
- queries: bfloat16 [16384, 8192], P('ctx', 'tp'), may hold values from -128 to 128
- cotangent: bfloat16 [16384, 8192], P('ctx', 'tp'), may hold values from -96 to 96
- image_keys: bfloat16 [64, 64, 1024], P('ctx', None, 'tp'), may hold values from -8 to 8
- image_values: bfloat16 [64, 64, 1024], P('ctx', None, 'tp'), may hold values from -6 to 6
- attn_gate: float32 [1], replicated, may hold values from 0.4 to 1.5
- block_mask: int32 [128, 64], P('ctx'), may hold values from 0 to 1, as said below
- image_owner: int32 [64], replicated, may hold values from 0 to 63, each once
Outputs:
- query_grad: bfloat16 [16384, 8192], P('ctx', 'tp')
- key_grad: bfloat16 [64, 64, 1024], P('ctx', None, 'tp')
- value_grad: bfloat16 [64, 64, 1024], P('ctx', None, 'tp')
- gate_grad: float32 [1], replicated
Inputs may be any that keep to these rules, and one draw needn't show every extreme that they name: `block_mask`: every text block reads at least one image; the 2 blocks of one index of ctx together read exactly 32 distinct images.
All inputs are finite; a program needn't handle non-finite values.
Results may differ from a plain program's by a relative error of at most 0.02.
Values may be sent and summed in bfloat16 or wider, within the bound.
A program may use at most 64 MiB of HBM per device.

v0:
```python
import math
import jax
import jax.numpy as jnp
from jax import lax
from jax.sharding import PartitionSpec as P

HD = 128
BLK = 128


def per_device(queries, cotangent, image_keys, image_values, attn_gate, block_mask, image_owner):
    tok_dev = queries.shape[0]
    local_kv = image_keys.shape[2] // HD
    local_heads = queries.shape[1] // HD
    groups = local_heads // local_kv
    img_tok = image_keys.shape[1]
    inv_root = 1.0 / math.sqrt(HD)
    read_most = lax.axis_size("ctx") // 2
    gathered_keys, gathered_values = (
        lax.all_gather(image_keys, "ctx", axis=0, tiled=True),
        lax.all_gather(image_values, "ctx", axis=0, tiled=True),
    )
    n_images = gathered_keys.shape[0]
    read_any = jnp.max(block_mask, axis=0)
    ranking = read_any * (2 * n_images) + (n_images - 1 - jnp.arange(n_images, dtype=jnp.int32))
    top_vals, image_ids = lax.top_k(ranking, read_most)
    is_read = read_any[image_ids] > 0
    slot_ids = image_owner[image_ids]
    block_keep = (block_mask[:, image_ids] > 0) & is_read[None, :]
    keep_mask = jnp.repeat(jnp.repeat(block_keep, BLK, axis=0), img_tok, axis=1)
    key_rows = jnp.take(gathered_keys, slot_ids, axis=0).reshape(read_most * img_tok, local_kv, HD)
    value_rows = jnp.take(gathered_values, slot_ids, axis=0).reshape(
        read_most * img_tok, local_kv, HD
    )
    query_heads = queries.reshape(tok_dev, local_kv, groups, HD).transpose(2, 0, 1, 3)
    cot_heads = cotangent.reshape(tok_dev, local_kv, groups, HD).transpose(2, 0, 1, 3)
    gate_value = jnp.tanh(attn_gate[0])

    def head_step(state_in, head_inputs):
        key_acc, value_acc, gate_acc = state_in
        query_one, cot_one = head_inputs
        scores = (
            jnp.einsum("tkd,skd->kts", query_one, key_rows, preferred_element_type=jnp.float32)
            * inv_root
        )
        scores = jnp.where(keep_mask, scores, -1e30)
        row_max = jnp.max(scores, axis=-1, keepdims=True)
        exp_terms = jnp.where(keep_mask, jnp.exp(scores - row_max), 0.0)
        prob_full = exp_terms / jnp.sum(exp_terms, axis=-1, keepdims=True)
        prob_half = prob_full.astype(jnp.bfloat16)
        attended = jnp.einsum(
            "kts,skd->tkd", prob_half, value_rows, preferred_element_type=jnp.float32
        )
        cot_f = cot_one.astype(jnp.float32)
        gate_part = jnp.sum(cot_f * attended)
        attn_grad = (gate_value * cot_f).astype(jnp.bfloat16)
        prob_grad = jnp.einsum(
            "tkd,skd->kts", attn_grad, value_rows, preferred_element_type=jnp.float32
        )
        row_delta = jnp.sum(attn_grad.astype(jnp.float32) * attended, axis=-1).T
        score_grad = (prob_full * (prob_grad - row_delta[:, :, None]) * inv_root).astype(
            jnp.bfloat16
        )
        query_grad = jnp.einsum(
            "kts,skd->tkd", score_grad, key_rows, preferred_element_type=jnp.float32
        ).astype(jnp.bfloat16)
        key_acc = key_acc + jnp.einsum(
            "kts,tkd->skd", score_grad, query_one, preferred_element_type=jnp.float32
        )
        value_acc = value_acc + jnp.einsum(
            "kts,tkd->skd", prob_half, attn_grad, preferred_element_type=jnp.float32
        )
        return ((key_acc, value_acc, gate_acc + gate_part), query_grad)

    zero_grads = jnp.zeros((read_most * img_tok, local_kv, HD), jnp.float32)
    init_state = (zero_grads, zero_grads, jnp.zeros((), jnp.float32))
    (key_acc, value_acc, gate_acc), head_grads = lax.scan(
        head_step, init_state, (query_heads, cot_heads)
    )
    query_grad = head_grads.transpose(1, 2, 0, 3).reshape(tok_dev, local_heads * HD)
    stacked = jnp.concatenate(
        [
            key_acc.reshape(read_most, img_tok, local_kv * HD),
            value_acc.reshape(read_most, img_tok, local_kv * HD),
        ],
        axis=-1,
    )
    stacked = jnp.where(is_read[:, None, None], stacked, 0.0)
    buffer = (
        jnp.zeros((n_images, img_tok, 2 * local_kv * HD), jnp.float32).at[slot_ids].add(stacked)
    )
    received = lax.all_to_all(buffer, "ctx", split_axis=0, concat_axis=0, tiled=True)
    summed = jnp.sum(received, axis=0, keepdims=True)
    key_grad = summed[:, :, : local_kv * HD].astype(jnp.bfloat16)
    value_grad = summed[:, :, local_kv * HD :].astype(jnp.bfloat16)
    gate_total = lax.psum(gate_acc, ("ctx", "tp"))
    term_count = tok_dev * lax.axis_size("ctx") * local_heads * lax.axis_size("tp") * HD
    gate_grad = ((1.0 - gate_value * gate_value) * gate_total / math.sqrt(term_count)).reshape(1)
    return (query_grad, key_grad, value_grad, gate_grad)


def solution(mesh):
    in_specs = (
        P("ctx", "tp"),
        P("ctx", "tp"),
        P("ctx", None, "tp"),
        P("ctx", None, "tp"),
        P(),
        P("ctx", None),
        P(),
    )
    out_specs = (P("ctx", "tp"), P("ctx", None, "tp"), P("ctx", None, "tp"), P())
    return jax.shard_map(
        per_device, mesh=mesh, in_specs=in_specs, out_specs=out_specs, check_vma=False
    )
```

profile of v0, /device:TPU:1, one launch (start us, length us, event | category | flops | bytes accessed | tf_op | source)
XLA Modules:
  0.0 885.6 jit_solution(12151461978923027463)
XLA Ops:
  10.9 2.0 top_k.11
  15.1 1.2 copy.35
  16.4 1.0 copy.36
  17.4 253.3 %all-gather.5.cloned.1.call-done = bf16[64,64,128]{2,1,0:T(8,128)(2,1)} async-done(((bf16[1,64,128]{2,1,0:T(8,128)(2,1)}), bf16[64,64,128]{2,1,0:T(8,128)(2,1)}) %all-gather.5.cloned.1.call-update) | async-done | bytes 1048592 | tf_op jit(solution)/shard_map/all_gather | solution.py:21
  270.7 1.9 gather_fusion.4
  272.6 297.7 %all-gather.3.cloned.1.call-done = bf16[64,64,128]{2,1,0:T(8,128)(2,1)} async-done(((bf16[1,64,128]{2,1,0:T(8,128)(2,1)}), bf16[64,64,128]{2,1,0:T(8,128)(2,1)}) %all-gather.3.cloned.1.call-update) | async-done | bytes 1048592 | tf_op jit(solution)/shard_map/all_gather | solution.py:20
  570.4 1.9 gather_fusion.3
  572.4 92.9 %while.17 = (s32[]{:T(128)}, f32[2048,1,128]{0,2,1:T(8,128)}, f32[2048,1,128]{0,2,1:T(8,128)}, f32[]{:T(128)}, bf16[8,256,1,128]{3,1,2,0:T(8,128)(2,1)}, /*index...) while((s32[]{:T(128)}, f32[2048,1,128]{0,2,1:T(8,128)}, ...), condition=%wide.region_7.9_spmd.clone, body=%wide.region_2.8_spmd.clone.sunk | while | flops 814710016 | bytes 48644448 | solution.py:77
  575.2 1.9 fusion.68
  577.8 1.4 fusion.69
  579.3 1.4 fusion.71
  580.7 1.1 fusion.72
  581.8 1.3 fusion.70
  583.1 1.0 copy-done.5
  586.8 1.9 fusion.68
  589.4 1.4 fusion.69
  590.9 1.4 fusion.71
  592.3 1.1 fusion.72
  593.4 1.3 fusion.70
  594.7 1.0 copy-done.5
  598.4 1.9 fusion.68
  601.0 1.4 fusion.69
  602.5 1.4 fusion.71
  603.9 1.1 fusion.72
  605.0 1.3 fusion.70
  606.3 1.0 copy-done.5
  610.1 1.9 fusion.68
  612.7 1.4 fusion.69
  614.1 1.4 fusion.71
  615.5 1.1 fusion.72
  616.6 1.3 fusion.70
  617.9 1.0 copy-done.5
  621.7 1.9 fusion.68
  624.3 1.4 fusion.69
  625.7 1.4 fusion.71
  627.1 1.1 fusion.72
  628.2 1.3 fusion.70
  629.5 1.0 copy-done.5
  633.3 1.9 fusion.68
  635.9 1.4 fusion.69
  637.3 1.4 fusion.71
  638.8 1.1 fusion.72
  639.8 1.3 fusion.70
  641.1 1.0 copy-done.5
  644.9 1.9 fusion.68
  647.5 1.4 fusion.69
  649.0 1.4 fusion.71
  650.4 1.1 fusion.72
  651.4 1.3 fusion.70
  652.7 1.0 copy-done.5
  656.5 1.9 fusion.68
  659.1 1.4 fusion.69
  660.6 1.4 fusion.71
  662.0 1.1 fusion.72
  663.1 1.3 fusion.70
  664.4 1.0 copy-done.5
  665.3 1.6 copy.40
  667.0 1.3 copy.41
  668.3 1.4 maximum_select_fusion
  669.8 2.5 broadcast_in_dim.68
  672.2 6.4 scatter_fusion
  678.6 7.4 all-to-all-start
  686.0 186.7 %psum.7 = f32[]{:T(128)} all-reduce(f32[]{:T(128)} %get-tuple-element.72), channel_id=1, replica_groups=mesh['ctx'=64,'tp'=8] {'ctx','tp'}, use_global_device_ids=true, to_apply=%region_10.12 | all-reduce | flops 1 | bytes 8 | tf_op jit(solution)/shard_map/psum | solution.py:96
  874.6 2.4 reduce_sum.36
  (165 shorter events, 29.4 us)
Async XLA Ops:
  7.2 6.5 copy-start
  7.2 9.2 %copy-start.8 = (bf16[256,1024]{1,0:T(8,128)(2,1)S(1)}, bf16[256,1024]{1,0:T(8,128)(2,1)}, u32[]{:S(2)}) copy-start(bf16[256,1024]{1,0:T(8,128)(2,1)} %param.12) | copy-start | bytes 1572868
  7.2 263.5 %all-gather.5.cloned.1.call-start = ((), (), s32[]{:S(2)}) async-start(), calls=%async_computation.2 | async-start | bytes 1064960 | tf_op jit(solution)/shard_map/all_gather | solution.py:21
  7.9 562.4 %all-gather.3.cloned.1.call-start = ((), (), s32[]{:S(2)}) async-start(), calls=%async_computation.1 | async-start | bytes 1064960 | tf_op jit(solution)/shard_map/all_gather | solution.py:20
  572.4 1.4 copy-start.6
  577.8 1.5 copy-start.1
  579.3 2.5 copy-start.4
  580.7 2.4 copy-start.2
  580.7 3.4 copy-start.7
  583.1 1.0 copy-start.5
  584.0 1.4 copy-start.6
  589.4 1.5 copy-start.1
  590.9 2.5 copy-start.4
  592.3 2.4 copy-start.2
  592.3 3.4 copy-start.7
  594.7 1.0 copy-start.5
  595.7 1.4 copy-start.6
  601.0 1.5 copy-start.1
  602.5 2.5 copy-start.4
  603.9 2.4 copy-start.2
  603.9 3.4 copy-start.7
  606.3 1.0 copy-start.5
  607.3 1.4 copy-start.6
  612.6 1.5 copy-start.1
  614.1 2.5 copy-start.4
  615.5 2.4 copy-start.2
  615.5 3.4 copy-start.7
  617.9 1.0 copy-start.5
  618.9 1.4 copy-start.6
  624.3 1.5 copy-start.1
  625.7 2.5 copy-start.4
  627.1 2.4 copy-start.2
  627.1 3.4 copy-start.7
  629.5 1.0 copy-start.5
  630.5 1.4 copy-start.6
  635.9 1.5 copy-start.1
  637.3 2.5 copy-start.4
  638.7 2.4 copy-start.2
  638.7 3.4 copy-start.7
  641.1 1.0 copy-start.5
  642.1 1.4 copy-start.6
  647.5 1.5 copy-start.1
  649.0 2.5 copy-start.4
  650.3 2.4 copy-start.2
  650.4 3.4 copy-start.7
  652.7 1.0 copy-start.5
  653.7 1.4 copy-start.6
  659.1 1.5 copy-start.1
  660.6 2.5 copy-start.4
  662.0 2.4 copy-start.2
  662.0 3.4 copy-start.7
  664.3 1.0 copy-start.5
  665.3 1.6 copy-start.3
  678.6 194.1 %copy-start.9 = (bf16[8,256,1,128]{3,1,2,0:T(8,128)(2,1)S(1)}, bf16[8,256,1,128]{3,1,2,0:T(8,128)(2,1)}, u32[]{:S(2)}) copy-start(bf16[8,256,1,128]{3,1,2,0:T(8,128)(2,1)} %get-tuple-element.69) | copy-start | bytes 1572868
  678.6 196.0 %all-to-all-start = ((f32[64,64,256]{2,1,0:T(8,128)}), f32[64,64,256]{2,1,0:T(8,128)}, u32[]{:S(2)}, u32[]{:S(2)}) async-start(f32[64,64,256]{2,1,0:T(8,128)} %scatter_fusion), calls=%async_computation | async-start | bytes 8388608 | tf_op jit(solution)/shard_map/all_to_all | solution.py:92
Sparse Core Ops, SparseCore 0:
  10.1 260.5 all-gather.4
  272.8 297.4 all-gather.2
where the time goes:
time: 887 us; the launch traced here: 886 us
  waiting for transfers between devices  552 us (62%)
  blocking collectives  187 us (21%)
  matrix products  61.8 us (7%)
  local copies, waits for them, and re-layouts  30.3 us (3%)
  other arithmetic  24.2 us (3%)
  between operations  16.7 us (2%)
    all_gather x1, waiting for transfers between devices, per_device(): lax.all_gather(image_keys, 'ctx', axis=0, tiled=True)  298 us
    all_gather x1, waiting for transfers between devices, per_device(): lax.all_gather(image_values, 'ctx', axis=0, tiled=True)  253 us
    psum x1, blocking collectives, per_device(): gate_total = lax.psum(gate_acc, ('ctx', 'tp'))  187 us
  transfers between devices with their start and end apart: 3, of which 2 were waited for; matrix products, arithmetic and copies ran while one was open for 1% of the time, Pallas kernels for 0%

commit v1 on v0

--- a/solution.py
+++ b/solution.py
@@ -17,7 +17,9 @@
     inv_root = 1.0 / math.sqrt(HD)
     read_most = lax.axis_size("ctx") // 2
     gathered_keys, gathered_values = (
-        lax.all_gather(image_keys, "ctx", axis=0, tiled=True),
+        jnp.concatenate(
+            lax.all_to_all(jnp.stack([image_keys] * lax.axis_size("ctx")), "ctx", 0, 0), axis=0
+        ),
         lax.all_gather(image_values, "ctx", axis=0, tiled=True),
     )
     n_images = gathered_keys.shape[0]

time: 887 us -> 601 us (0.68)
  waiting for transfers between devices: 552 us -> 251 us
  starting transfers between devices: 7.46 us -> 23 us
    all_gather x1 -> x0, waiting for transfers between devices: 298 us -> none  [per_device(): lax.all_gather(image_keys, 'ctx', axis=0, tiled=True)]
    all_gather x1, waiting for transfers between devices: 253 us -> 234 us  [per_device(): lax.all_gather(image_values, 'ctx', axis=0, tiled=True)]
    all_to_all x0 -> x1, waiting for transfers between devices: none -> 16.4 us  [per_device(): lax.all_to_all(jnp.stack([image_keys] * lax.axis_size('ctx')), 'ctx', 0, 0)]
    all_to_all x0 -> x1, starting transfers between devices: none -> 15.5 us  [per_device(): lax.all_to_all(jnp.stack([image_keys] * lax.axis_size('ctx')), 'ctx', 0, 0)]
where the time goes in v1:
time: 601 us; the launch traced here: 600 us
  waiting for transfers between devices  251 us (42%)
  blocking collectives  188 us (31%)
  matrix products  61.8 us (10%)
  local copies, waits for them, and re-layouts  29.4 us (5%)
  other arithmetic  23.5 us (4%)
  starting transfers between devices  23 us (4%)
  between operations  16.7 us (3%)
  loops' own time  6.11 us (1%)
    all_gather x1, waiting for transfers between devices, per_device(): lax.all_gather(image_values, 'ctx', axis=0, tiled=True)  234 us
    psum x1, blocking collectives, per_device(): gate_total = lax.psum(gate_acc, ('ctx', 'tp'))  188 us
    all_to_all x1, waiting for transfers between devices, per_device(): lax.all_to_all(jnp.stack([image_keys] * lax.axis_size('ctx')), 'ctx', 0, 0)  16.4 us
    dot_general x8, matrix products, head_step(): jnp.einsum('kts,skd->tkd', prob_half, value_rows, preferred_element_type=...  15.5 us
    all_to_all x1, starting transfers between devices, per_device(): lax.all_to_all(jnp.stack([image_keys] * lax.axis_size('ctx')), 'ctx', 0, 0)  15.5 us
  transfers between devices with their start and end apart: 3, of which 2 were waited for; matrix products, arithmetic and copies ran while one was open for 1% of the time, Pallas kernels for 0%

profile of v1, /device:TPU:1, one launch (start us, length us, event | category | flops | bytes accessed | tf_op | source)
XLA Modules:
  0.0 599.6 jit_solution(14130284305143471469)
XLA Ops:
  7.2 2.0 stack.2
  9.2 15.5 %all-to-all-start = ((bf16[64,1,64,128]{3,2,1,0:T(8,128)(2,1)}), bf16[64,1,64,128]{3,2,1,0:T(8,128)(2,1)S(1)}, u32[]{:S(2)}, u32[]{:S(2)}) async-start(bf16[64,1,64,128]{3,2,1,0:T(8,128)(2,1)} %stack.2), calls=%async_computation | async-start | bytes 2097152 | tf_op jit(solution)/shard_map/all_to_all | solution.py:21
  26.3 2.0 top_k.11
  30.8 1.0 copy.36
  31.8 16.4 %all-to-all-done = bf16[64,1,64,128]{3,2,1,0:T(8,128)(2,1)S(1)} async-done(((bf16[64,1,64,128]{3,2,1,0:T(8,128)(2,1)}), bf16[64,1,64,128]{3,2,1,0:T(8,128)(2,1)S(1)}, u32[]{:S(2)}, u32[]{:S(2)}) %all-to-all-start) | async-done | bytes 1048608 | tf_op jit(solution)/shard_map/all_to_all | solution.py:21
  48.9 233.9 %all-gather.2.cloned.1.call-done = bf16[64,64,128]{2,1,0:T(8,128)(2,1)} async-done(((bf16[1,64,128]{2,1,0:T(8,128)(2,1)}), bf16[64,64,128]{2,1,0:T(8,128)(2,1)}) %all-gather.2.cloned.1.call-update) | async-done | bytes 1048592 | tf_op jit(solution)/shard_map/all_gather | solution.py:23
  282.8 1.9 gather_fusion.4
  284.9 92.9 %while.17 = (s32[]{:T(128)}, f32[2048,1,128]{0,2,1:T(8,128)}, f32[2048,1,128]{0,2,1:T(8,128)}, f32[]{:T(128)}, bf16[8,256,1,128]{3,1,2,0:T(8,128)(2,1)}, /*index...) while((s32[]{:T(128)}, f32[2048,1,128]{0,2,1:T(8,128)}, ...), condition=%wide.region_7.9_spmd.clone, body=%wide.region_2.8_spmd.clone.sunk | while | flops 814710016 | bytes 48644448 | solution.py:79
  287.7 1.9 fusion.68
  290.3 1.4 fusion.69
  291.8 1.4 fusion.71
  293.2 1.1 fusion.72
  294.2 1.3 fusion.70
  295.5 1.0 copy-done.5
  299.3 1.9 fusion.68
  301.9 1.4 fusion.69
  303.4 1.4 fusion.71
  304.8 1.1 fusion.72
  305.9 1.3 fusion.70
  307.2 1.0 copy-done.5
  310.9 1.9 fusion.68
  313.5 1.4 fusion.69
  315.0 1.4 fusion.71
  316.4 1.1 fusion.72
  317.5 1.3 fusion.70
  318.8 1.0 copy-done.5
  322.5 1.9 fusion.68
  325.1 1.4 fusion.69
  326.6 1.4 fusion.71
  328.0 1.1 fusion.72
  329.1 1.3 fusion.70
  330.4 1.0 copy-done.5
  334.1 1.9 fusion.68
  336.8 1.4 fusion.69
  338.2 1.4 fusion.71
  339.6 1.1 fusion.72
  340.7 1.3 fusion.70
  342.0 1.0 copy-done.5
  345.8 1.9 fusion.68
  348.4 1.4 fusion.69
  349.8 1.4 fusion.71
  351.2 1.1 fusion.72
  352.3 1.3 fusion.70
  353.6 1.0 copy-done.5
  357.4 1.9 fusion.68
  360.0 1.4 fusion.69
  361.4 1.4 fusion.71
  362.8 1.1 fusion.72
  363.9 1.3 fusion.70
  365.2 1.0 copy-done.5
  369.0 1.9 fusion.68
  371.6 1.4 fusion.69
  373.1 1.4 fusion.71
  374.5 1.1 fusion.72
  375.5 1.3 fusion.70
  376.8 1.0 copy-done.5
  377.8 1.6 copy.40
  379.5 1.3 copy.41
  380.8 1.4 maximum_select_fusion
  382.2 2.5 broadcast_in_dim.68
  384.7 6.4 %scatter_fusion = f32[64,64,256]{2,1,0:T(8,128)} fusion(f32[64,64,256]{2,1,0:T(8,128)} %broadcast_in_dim.68, s32[32]{0:T(128)S(1)} %fusion.36, f32[32,64,256]{2,1,0:T(8,128)S(1)} %maximum_select_fusion), kind=kCustom, calls=%fused_computation.5 | custom fusion | flops 524288 | bytes 6291584 | tf_op jit(solution)/shard_map/scatter-add | solution.py:92
  391.1 7.5 %all-to-all-start.1 = ((f32[64,64,256]{2,1,0:T(8,128)}), f32[64,64,256]{2,1,0:T(8,128)}, u32[]{:S(2)}, u32[]{:S(2)}) async-start(f32[64,64,256]{2,1,0:T(8,128)} %scatter_fusion), calls=%async_computation.1 | async-start | bytes 8388608 | tf_op jit(solution)/shard_map/all_to_all | solution.py:94
  398.6 188.1 %psum.7 = f32[]{:T(128)} all-reduce(f32[]{:T(128)} %get-tuple-element.72), channel_id=1, replica_groups=mesh['ctx'=64,'tp'=8] {'ctx','tp'}, use_global_device_ids=true, to_apply=%region_10.12 | all-reduce | flops 1 | bytes 8 | tf_op jit(solution)/shard_map/psum | solution.py:98
  588.6 2.4 reduce_sum.36
  (169 shorter events, 28.2 us)
Async XLA Ops:
  7.2 21.9 %copy-start = (s32[64]{0:T(128)S(1)}, s32[64]{0:T(128)}, u32[]{:S(2)}) copy-start(s32[64]{0:T(128)} %param.17) | copy-start | bytes 772
  7.2 19.0 %copy-start.11 = (s32[2,64]{1,0:T(2,128)S(1)}, s32[2,64]{1,0:T(2,128)}, u32[]{:S(2)}) copy-start(s32[2,64]{1,0:T(2,128)} %param.16) | copy-start | bytes 1540
  7.2 23.4 %copy-start.8 = (bf16[256,1024]{1,0:T(8,128)(2,1)S(1)}, bf16[256,1024]{1,0:T(8,128)(2,1)}, u32[]{:S(2)}) copy-start(bf16[256,1024]{1,0:T(8,128)(2,1)} %param.11) | copy-start | bytes 1572868
  9.2 21.6 %copy-start.9 = (bf16[256,1024]{1,0:T(8,128)(2,1)S(1)}, bf16[256,1024]{1,0:T(8,128)(2,1)}, u32[]{:S(2)}) copy-start(bf16[256,1024]{1,0:T(8,128)(2,1)} %param.12) | copy-start | bytes 1572868
  9.2 39.0 %all-to-all-start = ((bf16[64,1,64,128]{3,2,1,0:T(8,128)(2,1)}), bf16[64,1,64,128]{3,2,1,0:T(8,128)(2,1)S(1)}, u32[]{:S(2)}, u32[]{:S(2)}) async-start(bf16[64,1,64,128]{3,2,1,0:T(8,128)(2,1)} %stack.2), calls=%async_computation | async-start | bytes 2097152 | tf_op jit(solution)/shard_map/all_to_all | solution.py:21
  24.7 258.1 %all-gather.2.cloned.1.call-start = ((), (), s32[]{:S(2)}) async-start(), calls=%async_computation.2 | async-start | bytes 1064960 | tf_op jit(solution)/shard_map/all_gather | solution.py:23
  284.9 1.4 copy-start.6
  290.3 1.4 copy-start.1
  291.8 2.5 copy-start.4
  293.1 2.4 copy-start.2
  293.2 3.4 copy-start.7
  295.5 1.0 copy-start.5
  296.5 1.4 copy-start.6
  301.9 1.5 copy-start.1
  303.4 2.5 copy-start.4
  304.8 2.4 copy-start.2
  304.8 3.4 copy-start.7
  307.1 1.0 copy-start.5
  308.1 1.4 copy-start.6
  313.5 1.5 copy-start.1
  315.0 2.5 copy-start.4
  316.4 2.4 copy-start.2
  316.4 3.4 copy-start.7
  318.8 1.0 copy-start.5
  319.8 1.4 copy-start.6
  325.1 1.5 copy-start.1
  326.6 2.5 copy-start.4
  328.0 2.4 copy-start.2
  328.0 3.4 copy-start.7
  330.4 1.0 copy-start.5
  331.4 1.4 copy-start.6
  336.7 1.5 copy-start.1
  338.2 2.5 copy-start.4
  339.6 2.4 copy-start.2
  339.6 3.4 copy-start.7
  342.0 1.0 copy-start.5
  343.0 1.4 copy-start.6
  348.4 1.5 copy-start.1
  349.8 2.5 copy-start.4
  351.2 2.4 copy-start.2
  351.2 3.4 copy-start.7
  353.6 1.0 copy-start.5
  354.6 1.4 copy-start.6
  360.0 1.5 copy-start.1
  361.4 2.5 copy-start.4
  362.8 2.4 copy-start.2
  362.8 3.4 copy-start.7
  365.2 1.0 copy-start.5
  366.2 1.4 copy-start.6
  371.6 1.5 copy-start.1
  373.0 2.5 copy-start.4
  374.4 2.4 copy-start.2
  374.4 3.4 copy-start.7
  376.8 1.0 copy-start.5
  377.8 1.6 copy-start.3
  391.1 195.6 %copy-start.10 = (bf16[8,256,1,128]{3,1,2,0:T(8,128)(2,1)S(1)}, bf16[8,256,1,128]{3,1,2,0:T(8,128)(2,1)}, u32[]{:S(2)}) copy-start(bf16[8,256,1,128]{3,1,2,0:T(8,128)(2,1)} %get-tuple-element.69) | copy-start | bytes 1572868
  391.1 197.5 %all-to-all-start.1 = ((f32[64,64,256]{2,1,0:T(8,128)}), f32[64,64,256]{2,1,0:T(8,128)}, u32[]{:S(2)}, u32[]{:S(2)}) async-start(f32[64,64,256]{2,1,0:T(8,128)} %scatter_fusion), calls=%async_computation.1 | async-start | bytes 8388608 | tf_op jit(solution)/shard_map/all_to_all | solution.py:94
Sparse Core Ops, SparseCore 0:
  27.6 255.1 all-gather.1
